TPU v7x, 32 devices: a whole 2x2x4 slice. The times are simulated.
32 devices in a mesh: batch: 8 (over y, x, core), seq: 4 (over z).
Axes of the slice: x: 2, y: 2, z: 4, core: 2. Of those that a mesh axis runs over, the one named last changes fastest.
Arguments:
- inputs: bfloat16 [32, 2048, 768], P('batch', 'seq'), may hold values from -6 to 6
- cotangent: bfloat16 [32, 2048, 768], P('batch', 'seq'), may hold values from -12 to 12
- set_kind: int32 [32], P('batch'), may hold values from 0 to 1, as said below
- row_offset: int32 [32, 4], P('batch'), may hold values from 0 to 1536, as said below
- query_w: bfloat16 [768, 768], replicated, may hold values from -0.21875 to 0.21875
- key_w: bfloat16 [768, 768], replicated, may hold values from -0.21875 to 0.21875
- value_w: bfloat16 [768, 768], replicated, may hold values from -0.21875 to 0.21875
- output_w: bfloat16 [768, 768], replicated, may hold values from -0.875 to 0.875
- up_w: bfloat16 [768, 3072], replicated, may hold values from -0.21875 to 0.21875
- down_w: bfloat16 [3072, 768], replicated, may hold values from -0.109375 to 0.109375
- compress: bfloat16 [2048, 256], replicated, may hold values from -0.1875 to 0.1875
- first_gain: float32 [768], replicated, may hold values from 0.1 to 1.9
- first_bias: float32 [768], replicated, may hold values from -3 to 3
- second_gain: float32 [768], replicated, may hold values from 0.1 to 1.9
- second_bias: float32 [768], replicated, may hold values from -3 to 3
Outputs:
- layer_out: bfloat16 [32, 2048, 768], P('batch', 'seq')
- input_grad: float32 [32, 2048, 768], P('batch', 'seq')
- query_grad: float32 [768, 768], P('batch', 'seq')
- key_grad: float32 [768, 768], P('batch', 'seq')
- value_grad: float32 [768, 768], P('batch', 'seq')
- output_grad: float32 [768, 768], P('batch', 'seq')
- up_grad: float32 [768, 3072], P('batch', 'seq')
- down_grad: float32 [3072, 768], P('batch', 'seq')
- compress_grad: float32 [2048, 256], replicated
- first_gain_grad: float32 [768], replicated
- first_bias_grad: float32 [768], replicated
- second_gain_grad: float32 [768], replicated
- second_bias_grad: float32 [768], replicated
Inputs may be any that keep to these rules, and one draw needn't show every extreme that they name: `set_kind`: the 4 consecutive sets of each batch index include at least one set that is a single sequence. `row_offset`: entries of a set that is a single sequence are not read.
All inputs are finite; a program needn't handle non-finite values.
Results may differ from a plain program's by a relative error of at most 0.028.
Values may be sent and summed in bfloat16 or wider, within the bound.
A program may use at most 256 MiB of HBM per device.

v0:
```python
import functools

import jax
import jax.numpy as jnp
from jax import lax
from jax.experimental import pallas as pl
from jax.experimental.pallas import tpu as pltpu
from jax.sharding import PartitionSpec as P

DH = 64
LANES = 128
TILE = 8
SCALE = DH ** (-0.5)
EPS = 1e-05
MESH = pl.DeviceIdType.MESH
VMEM_LIMIT = 63 * 1024 * 1024
bf16 = jnp.bfloat16
f32 = jnp.float32


def dot(left, right):
    return lax.dot_general(left, right, (((1,), (0,)), ((), ())), preferred_element_type=f32)


def dot_nt(left, right):
    return lax.dot_general(left, right, (((1,), (1,)), ((), ())), preferred_element_type=f32)


def dot_tn(left, right):
    return lax.dot_general(left, right, (((0,), (0,)), ((), ())), preferred_element_type=f32)


def params(**more):
    return pltpu.CompilerParams(vmem_limit_bytes=VMEM_LIMIT, **more)


def whole(shape):
    return pl.BlockSpec(shape, lambda *_: (0,) * len(shape), pipeline_mode=pl.Buffered(1))


def per_set(shape):
    return pl.BlockSpec((1,) + tuple(shape), lambda s, *_: (s,) + (0,) * len(shape))


def own_start(kinds, offsets, at, row_count, shortest):
    position = lax.axis_index("seq") * row_count
    return jnp.where(kinds[at] > 0, position, offsets[at, position // shortest] + position % shortest)


def aligned(start):
    begin = start // TILE * TILE
    return pl.multiple_of(begin, TILE), start - begin


def place():
    batch = lax.axis_index("batch")
    return batch // 4, batch // 2 % 2, batch % 2, lax.axis_index("seq")


def device(y, x, core, z):
    return ((y * 2 + x) * 2 + core, z)


def greet(others):
    barrier = pltpu.get_barrier_semaphore()
    for other in others:
        pl.semaphore_signal(barrier, inc=1, device_id=other, device_id_type=MESH)
    pl.semaphore_wait(barrier, len(others))


def remote(src, dst, send_sem, recv_sem, target):
    return pltpu.make_async_remote_copy(src, dst, send_sem, recv_sem, device_id=target, device_id_type=MESH)


class LineSum:
    def __init__(self, line, lag, own, from_left, from_right, sems):
        y, x, core, self.z = place()
        self.line, self.lag, self.own = line, lag, own
        self.right = device(y, x, core, (self.z + 1) % line)
        self.left = device(y, x, core, (self.z + line - 1) % line)
        inner, outer = self.z > 0, self.z < line - 1
        self.ways = (
            (from_left, self.right, inner, outer, sems[0], sems[1]),
            (from_right, self.left, outer, inner, sems[2], sems[3]),
        )

    def greet(self):
        barrier = pltpu.get_barrier_semaphore()
        for way in self.ways:

            @pl.when(way[3])
            def _():
                pl.semaphore_signal(barrier, inc=1, device_id=way[1], device_id_type=MESH)

        both = jnp.logical_and(self.z > 0, self.z < self.line - 1).astype(jnp.int32)
        pl.semaphore_wait(barrier, 1 + both)

    def prepare(self):
        for way in self.ways:

            @pl.when(jnp.logical_not(way[2]))
            def _():
                way[0][...] = jnp.zeros_like(way[0])

    def copy(self, way, at):
        held, target, _, _, send, recv = way
        return remote(held.at[at], held.at[at], send.at[at], recv.at[at], target)

    def forward(self, way, at):
        @pl.when(way[2])
        def _():
            self.copy(way, at).wait_recv()

        way[0][at] = way[0][at] + self.own[at]

        @pl.when(way[3])
        def _():
            self.copy(way, at).start()

    def slots(self):
        return self.own.shape[0] + self.lag * (self.line - 1)

    def serve(self, slot):
        for way, hops in zip(self.ways, (self.z, self.line - 1 - self.z)):
            at = slot - self.lag * hops

            @pl.when(jnp.logical_and(at >= 0, at < self.own.shape[0]))
            def _():
                self.forward(way, at)

    def serve_many(self, begin, count):
        def slot(at, carry):
            self.serve(at)
            return carry

        lax.fori_loop(begin, begin + count, slot, 0)

    def total(self, at, joined):
        own = self.own[at].astype(f32)
        both = self.ways[0][0][at].astype(f32) + self.ways[1][0][at].astype(f32)
        return jnp.where(joined, both - own, own).astype(bf16)

    def finish(self):
        for way in self.ways:

            @pl.when(way[3])
            def _():
                def wait(at, carry):
                    self.copy(way, at).wait_send()
                    return carry

                lax.fori_loop(0, self.own.shape[0], wait, 0)


class Scatter:
    def __init__(self, x_first, part, from_core, from_first, from_second, send, recv):
        y, x, core, z = place()
        self.part, self.recvs = part, (from_core, from_first, from_second)
        along_x, along_y = device(y, 1 - x, core, z), device(1 - y, x, core, z)
        self.core, self.x, self.y, self.x_first = core, x, y, x_first
        if x_first:
            sources = (part.at[:, :, 1 - core], from_core.at[:, 1 - x], from_first.at[1 - y])
            targets = (device(y, x, 1 - core, z), along_x, along_y)
        else:
            sources = (part.at[:, :, 1 - core], from_core.at[1 - y], from_first.at[1 - x])
            targets = (device(y, x, 1 - core, z), along_y, along_x)
        self.copies = [
            remote(sources[i], self.recvs[i], send.at[i], recv.at[i], targets[i]) for i in range(3)
        ]

    def start(self):
        self.copies[0].start()

    def first(self):
        self.copies[0].wait()
        self.recvs[0][...] = self.recvs[0][...] + self.part[:, :, self.core]
        self.copies[1].start()

    def second(self):
        self.copies[1].wait_recv()
        kept = self.recvs[0][:, self.x] if self.x_first else self.recvs[0][self.y]
        self.recvs[1][...] = self.recvs[1][...] + kept
        self.copies[2].start()

    def done(self):
        self.copies[2].wait_recv()
        kept = self.recvs[1][self.y] if self.x_first else self.recvs[1][self.x]
        return self.recvs[2][...].astype(f32) + kept.astype(f32)

    def finish(self):
        for copy in self.copies[1:]:
            copy.wait_send()


class LineScatter:
    def __init__(self, blocks, near, far, send, recv):
        y, x, core, z = place()
        self.blocks, self.near, self.far = blocks, near, far
        self.high, self.low = z // 2, z % 2
        self.copies = [
            remote(blocks.at[:, 1 - self.low], near, send.at[0], recv.at[0], device(y, x, core, z + 1 - 2 * self.low)),
            remote(near.at[1 - self.high], far, send.at[1], recv.at[1], device(y, x, core, (z + 2) % 4)),
        ]

    def start(self):
        self.copies[0].start()

    def middle(self):
        self.copies[0].wait_recv()
        self.near[...] = self.near[...] + self.blocks[:, self.low]
        self.copies[1].start()

    def done(self):
        self.copies[1].wait_recv()
        return self.near[self.high].astype(f32) + self.far[...].astype(f32)

    def finish(self):
        for copy in self.copies:
            copy.wait_send()


def line_scatter_blocks(blocks, rows, line):
    step = rows.shape[1] // line
    for z in range(line):
        mine = rows[:, z * step : (z + 1) * step]
        if step % LANES:
            top = rows.shape[0] // 2
            mine = jnp.concatenate([mine[:top], mine[top:]], axis=1)
        blocks[z // 2, z % 2] = mine.astype(bf16)


def unfold(total, out):
    if total.shape[1] == out.shape[1]:
        out[...] = total
    else:
        top, step = total.shape[0], out.shape[1]
        out[:top, :] = total[:, :step]
        out[top:, :] = total[:, step:]


def block_shape(rows, width, line):
    step = width // line
    return (rows, step) if step % LANES == 0 else (rows // 2, step * 2)


def grad_columns(part, left, right):
    step = 2 * LANES

    def columns(j, carry):
        span = pl.ds(pl.multiple_of(j * step, LANES), step)
        part[:, span] = dot_tn(left(), right(span)).astype(bf16)
        return carry

    lax.fori_loop(0, part.shape[-1] // step, columns, 0)


def scatter_scratch(rows, width, *count):
    shapes = [(2, 2, rows, width), (2, rows, width), (rows, width)]
    return [pltpu.VMEM(count + shape, bf16) for shape in shapes] + [pltpu.SemaphoreType.DMA(count + (3,))] * 2


def line_scratch(rows, width, line):
    block = block_shape(rows, width, line)
    return [pltpu.VMEM(n + block, bf16) for n in ((2, 2), (2,), ())] + [pltpu.SemaphoreType.DMA((2,))] * 2


class Neighbours:
    def __init__(self, line):
        y, x, core, z = place()
        self.core = device(y, x, 1 - core, z)
        places = [((y + dy) % 2, (x + dx) % 2) for dy, dx in ((0, 1), (1, 0), (1, 1))]
        self.plane = [(py * 2 + px, device(py, px, core, z)) for py, px in places]
        self.line = [((z + d) % line, device(y, x, core, (z + d) % line)) for d in range(1, line)]

    def everyone(self):
        return [self.core] + [to for _, to in self.plane] + [to for _, to in self.line]


class Total:
    counts = lambda line: (2, 6, 2 * (line - 1), line - 1, 3, 1)

    def __init__(self, line, near, table, norms, table_out, norms_out, mine, from_core, from_plane, from_line, gathered,
                 core_norms, plane_norms, line_norms, *sems):
        y, x, core, z = place()
        plane = y * 2 + x
        pairs = [(sems[2 * i], sems[2 * i + 1]) for i in range(6)]
        self.running = []

        def start(stage, moves):
            send, recv = pairs[stage]
            self.running = [remote(src, dst, send.at[i], recv.at[i], to) for i, (src, dst, to) in enumerate(moves)]
            for copy in self.running:
                copy.start()

        def to_core():
            mine[...] = table[...]
            core_norms[0] = norms[...]
            start(0, [(mine.at[1 - core], from_core, near.core), (core_norms.at[0], core_norms.at[1], near.core)])

        def to_plane():
            from_core[...] = from_core[...] + mine[core]
            plane_norms[plane] = core_norms[0] + core_norms[1]
            kept = plane_norms.at[plane]
            start(1, [(from_core.at[p], from_plane.at[i], to) for i, (p, to) in enumerate(near.plane)]
                  + [(kept, kept, to) for _, to in near.plane])

        def to_line():
            total = from_core[plane].astype(f32)
            for i in range(3):
                total = total + from_plane[i].astype(f32)
            mine[0, 0] = total.astype(bf16)
            line_norms[z] = plane_norms[0] + plane_norms[1] + plane_norms[2] + plane_norms[3]
            kept = line_norms.at[z]
            start(2, [(mine.at[0, 0, p], from_line.at[i], to) for i, (p, to) in enumerate(near.line)]
                  + [(kept, kept, to) for _, to in near.line])

        def back_line():
            total = mine[0, 0, z].astype(f32)
            for i in range(line - 1):
                total = total + from_line[i].astype(f32)
            gathered[core, plane, z] = total.astype(bf16)
            all_norms = line_norms[0]
            for i in range(1, line):
                all_norms = all_norms + line_norms[i]
            norms_out[...] = all_norms
            block = gathered.at[core, plane, z]
            start(3, [(block, block, to) for _, to in near.line])

        def back_plane():
            block = gathered.at[core, plane]
            start(4, [(block, block, to) for _, to in near.plane])

        def back_core():
            block = gathered.at[core]
            start(5, [(block, block, near.core)])

        def close():
            table_out[...] = gathered[...]

        self.stages = [to_core, to_plane, to_line, back_line, back_plane, back_core, close]

    def advance(self):
        for copy in self.running:
            copy.wait()
        self.running = []
        self.stages.pop(0)()

    @staticmethod
    def scratch(line, shape, norms):
        vmem = pltpu.VMEM
        return [
            vmem(shape, bf16), vmem(shape[1:], bf16), vmem((3,) + shape[2:], bf16), vmem((line - 1,) + shape[3:], bf16),
            vmem(shape, bf16), vmem((2,) + norms, f32), vmem((4,) + norms, f32), vmem((line,) + norms, f32),
        ] + [pltpu.SemaphoreType.DMA((n,)) for n in Total.counts(line) for _ in range(2)]


def closing_kernel(line, table_ref, norms_ref, up_ref, down_ref, square_any,
                   table_out, norms_out, up_out, down_out, square_out, square_part, load_sems, *scratch):
    scratch = list(scratch)
    take = lambda n: [scratch.pop(0) for _ in range(n)]
    pairs = [(square_any.at[i], square_part.at[i]) for i in range(3)]
    loads = [pltpu.make_async_copy(src, dst, load_sems.at[i]) for i, (src, dst) in enumerate(pairs)]
    for load in loads:
        load.start()
    near = Neighbours(line)
    greet(near.everyone())
    total = Total(line, near, table_ref, norms_ref, table_out, norms_out, *take(8 + 12))
    total.advance()
    query, key, value = [Scatter(i != 1, square_part.at[i], *take(5)) for i in range(3)]
    square_lines = [LineScatter(*take(5)) for _ in range(3)]
    for load, job in zip(loads, (query, key, value)):
        load.wait()
        job.start()
    across = []
    for rows, out in ((up_ref, up_out), (down_ref, down_out)):
        for chunk in range(rows.shape[0]):
            job = LineScatter(*take(5))
            line_scatter_blocks(job.blocks, rows[chunk], line)
            job.start()
            across.append((job, out.at[chunk]))
    total.advance()
    query.first()
    key.first()
    value.first()
    for job, _ in across:
        job.middle()
    total.advance()
    query.second()
    total.advance()
    key.second()
    for job, out in across:
        unfold(job.done(), out)
    total.advance()
    value.second()
    jobs = [(job, square_lines[i], square_out.at[i]) for i, job in enumerate((query, key, value))]
    for job, line_job, _ in jobs:
        line_scatter_blocks(line_job.blocks, job.done(), line)
        line_job.start()
    total.advance()
    for _, line_job, _ in jobs:
        line_job.middle()
    total.advance()
    for _, line_job, out in jobs:
        unfold(line_job.done(), out)
    for job, _ in across:
        job.finish()
    for job, line_job, _ in jobs:
        job.finish()
        line_job.finish()


def closing(table, norms, up_rows, down_rows, squares):
    line = lax.axis_size("seq")
    longest, comp = table.shape
    shape = (2, 4, line, longest // (8 * line), comp)
    vmem, anywhere = pl.BlockSpec(memory_space=pltpu.VMEM), pl.BlockSpec(memory_space=pl.ANY)
    out = lambda *dims: jax.ShapeDtypeStruct(dims, f32)
    (ups, rows, wide), (downs, tall, width), count = up_rows.shape, down_rows.shape, squares.shape[0]
    squares = squares.reshape(count, 2, 2, 2, rows, width)
    scratch = [pltpu.VMEM(squares.shape, bf16), pltpu.SemaphoreType.DMA((count,))]
    scratch += Total.scratch(line, shape, norms.shape)
    scratch += scatter_scratch(rows, width) * count + line_scratch(rows, width, line) * count
    scratch += line_scratch(rows, wide, line) * ups + line_scratch(tall, width, line) * downs
    return pl.pallas_call(
        functools.partial(closing_kernel, line),
        in_specs=[vmem] * 4 + [anywhere],
        out_specs=[vmem] * 5,
        out_shape=[
            jax.ShapeDtypeStruct(shape, bf16), out(*norms.shape), out(ups, rows, wide // line),
            out(downs, tall, width // line), out(count, rows, width // line),
        ],
        scratch_shapes=scratch,
        compiler_params=params(collective_id=3, has_side_effects=True),
        name="closing",
    )(table.reshape(shape), norms, up_rows, down_rows, squares)


def front_kernel(start_ref, compress_ref, x_ref, wq_ref, table_ref, c_ref, q_ref, wide):
    step = pl.program_id(0)

    longest = compress_ref.shape[0]

    @pl.when(step == 0)
    def _():
        wide[:longest, :] = compress_ref[...].astype(f32)
        wide[longest:, :] = jnp.zeros((TILE, wide.shape[1]), f32)

    rows = x_ref.shape[1]
    begin, shift = aligned(start_ref[step])
    window = wide[pl.ds(begin, rows + TILE), :]
    table = pltpu.roll(window, lax.rem(rows + TILE - shift, rows + TILE), 0)[:rows].astype(bf16)
    table_ref[0] = table
    x = x_ref[0]
    c_ref[0] = dot_tn(table, x).astype(bf16)
    q_ref[0] = (dot(x, wq_ref[...]) * SCALE).astype(bf16)


def front(starts, compress, x, wq):
    sets, rows, width = x.shape
    longest, comp = compress.shape
    grid_spec = pltpu.PrefetchScalarGridSpec(
        num_scalar_prefetch=1,
        grid=(sets,),
        in_specs=[whole(compress.shape), per_set((rows, width)), whole(wq.shape)],
        out_specs=[per_set((rows, comp)), per_set((comp, width)), per_set((rows, width))],
        scratch_shapes=[pltpu.VMEM((longest + TILE, comp), f32)],
    )
    return pl.pallas_call(
        front_kernel,
        grid_spec=grid_spec,
        out_shape=[
            jax.ShapeDtypeStruct((sets, rows, comp), bf16),
            jax.ShapeDtypeStruct((sets, comp, width), bf16),
            jax.ShapeDtypeStruct((sets, rows, width), bf16),
        ],
        compiler_params=params(),
        name="front",
    )(starts, compress, x, wq)


def head_blocks(pair, first_half):
    zero = jnp.zeros_like(pair)
    return jnp.concatenate([jnp.where(first_half, pair, zero), jnp.where(first_half, zero, pair)], axis=0)


def norm_forward(v):
    average = jnp.mean(v, axis=-1, keepdims=True)
    centered = v - average
    variance = jnp.mean(centered * centered, axis=-1, keepdims=True)
    inverse = lax.rsqrt(variance + EPS)
    return centered * inverse, inverse


def norm_backward(dz, z, inverse):
    return (dz - jnp.mean(dz, axis=-1, keepdims=True) - z * jnp.mean(dz * z, axis=-1, keepdims=True)) * inverse


PIECES = 4
LAG = 2
HALVES = 2


def layer_kernel(
    line, long_ref, offset_ref, compress_ref, c_ref, x_any, cot_ref, gain1_ref, bias1_ref, gain2_ref, bias2_ref, wq_any, wk_any, wv_any, wo_any, up_any, down_any,
    kc_ref, vc_ref, csum_ref, mixed_ref, hidden_ref, out_ref, gdown_ref, gatt_ref, go_ref, table_any, q_any,
    e_any, act_any, gup_any, output_grad_ref, sums_ref,
    xs, qs, wq, wk, wv, wo, up, down, e_buf, act, gup, z_first, rinv_ref, held, output_grad, weight_sems, x_sems, out_sems,
    *linked,
):
    step = pl.program_id(0)
    last = pl.num_programs(0) - 1
    sets, rows, width = xs.shape
    comp = kc_ref.shape[1]
    units = up.shape[1]
    chunk = 768
    loads = [
        pltpu.make_async_copy(src, dst, weight_sems.at[i])
        for i, (src, dst) in enumerate(
            ((wq_any, wq), (wk_any, wk), (wv_any, wv), (wo_any, wo), (up_any, up), (down_any, down))
        )
    ]
    x_loads = [pltpu.make_async_copy(x_any.at[s], xs.at[s], x_sems.at[s]) for s in range(sets)]
    q_store = pltpu.make_async_copy(qs, q_any, out_sems.at[3])
    e_store = pltpu.make_async_copy(e_buf, e_any.at[step], out_sems.at[0])
    act_store = pltpu.make_async_copy(act, act_any.at[step], out_sems.at[1])
    gup_store = pltpu.make_async_copy(gup, gup_any.at[step], out_sems.at[2])

    if line:
        tables, own, from_left, from_right, table_sems, *sems = linked
        sums = LineSum(line, LAG, own, from_left, from_right, sems)
        ahead = PIECES + LAG * (line - 1)
        t_stores = [pltpu.make_async_copy(tables.at[s], table_any.at[s], table_sems.at[s]) for s in range(sets)]

    def first_use(load):
        @pl.when(step == 0)
        def _():
            load.wait()

    @pl.when(step == 0)
    def _():
        for load in x_loads:
            load.start()
        sums_ref[...] = jnp.zeros_like(sums_ref)
        output_grad[...] = jnp.zeros_like(output_grad)
        if line:
            longest = compress_ref.shape[0]
            sums.greet()
            sums.prepare()
            grid = (rows, rows)
            ahead_by = lax.broadcasted_iota(jnp.int32, grid, 1) - lax.broadcasted_iota(jnp.int32, grid, 0)

        def summarize(s, carry):
            pltpu.make_async_copy(x_any.at[s], xs.at[s], x_sems.at[s]).wait()

            @pl.when(s == 0)
            def _():
                loads[0].start()

            if line:
                table = jnp.zeros((rows, comp), f32)
                start = own_start(long_ref, offset_ref, s, rows, longest // 4)
                for at in range(0, longest, rows):
                    chosen = jnp.where(ahead_by == start - at, 1.0, 0.0).astype(bf16)
                    table = table + dot(chosen, compress_ref[at : at + rows, :])
                table = table.astype(bf16)
                tables[s] = table
                pltpu.make_async_copy(tables.at[s], table_any.at[s], table_sems.at[s]).start()
                c = dot_tn(table, xs[s]).astype(bf16)
                own[pl.ds(s * PIECES, PIECES)] = c.reshape(PIECES, comp // PIECES, width)
                sums.serve(s)
            return carry

        lax.fori_loop(0, sets, summarize, 0)
        for load in loads[1:]:
            load.start()
        loads[0].wait()

        def query(s, carry):
            qs[s] = (dot(xs[s], wq[...]) * SCALE).astype(bf16)
            if line:
                sums.serve(sets + s)
            return carry

        lax.fori_loop(0, sets, query, 0)
        q_store.start()
        if line:
            sums.serve_many(2 * sets, ahead - 2 * sets)

    def serve(part):
        if line:
            count = PIECES // 4

            @pl.when(step < last)
            def _():
                sums.serve_many(ahead + step * PIECES + part * count, count)

    if line:
        joined = long_ref[step] > 0
        for piece in range(PIECES):
            size = comp // PIECES
            csum_ref[0, piece * size : (piece + 1) * size, :] = sums.total(step * PIECES + piece, joined)
    else:
        csum_ref[0] = c_ref[0]
    first_use(loads[1])
    first_use(loads[2])
    c = csum_ref[0]
    kc_ref[0] = dot(c, wk[...]).astype(bf16)
    vc_ref[0] = dot(c, wv[...]).astype(bf16)
    half = lax.broadcasted_iota(jnp.int32, (comp, LANES), 1) < DH
    ones = head_blocks(jnp.ones((comp, LANES), bf16), half)

    @pl.when(step > 0)
    def _():
        e_store.wait()

    def attend(pair):
        lanes = pl.ds(pl.multiple_of(pair * LANES, LANES), LANES)
        keys = head_blocks(kc_ref[0, :, lanes], half)
        values = jnp.concatenate([head_blocks(vc_ref[0, :, lanes], half), ones], axis=1)
        scores = dot_nt(qs[step, :, lanes], keys)
        parts = []
        for head in range(2):
            mine = scores[:, head * comp : (head + 1) * comp]
            top = jnp.max(mine, axis=-1, keepdims=True)
            parts.append(jnp.exp(mine - top).astype(bf16))
        e = jnp.concatenate(parts, axis=1)
        e_buf[:, pl.ds(pl.multiple_of(pair * 2 * comp, LANES), 2 * comp)] = e
        total = dot(e, values)
        rinv = 1.0 / total[:, LANES:]
        rinv_ref[:, lanes] = rinv
        mixed_ref[0, :, lanes] = (total[:, :LANES] * rinv).astype(bf16)

    pairs = width // LANES // 2

    def some_heads(half_at, carry):
        for i in range(pairs):
            attend(half_at * pairs + i)
        return carry

    lax.fori_loop(0, 2, some_heads, 0)
    e_store.start()
    first_use(loads[3])
    serve(0)
    gain1, bias1, gain2, bias2 = (ref[...].reshape(1, width) for ref in (gain1_ref, bias1_ref, gain2_ref, bias2_ref))
    size = rows // HALVES
    halves = [pl.ds(h * size, size) for h in range(HALVES)]
    inverse1 = []
    for part in halves:
        z1, inv1 = norm_forward(xs[step, part, :].astype(f32) + dot(mixed_ref[0, part, :], wo[...]))
        inverse1.append(inv1)
        z_first[part, :] = z1
        hidden = z1 * gain1 + bias1
        hidden_ref[0, part, :] = hidden.astype(bf16)
        held[part, :] = hidden
    first_use(loads[4])
    first_use(loads[5])

    @pl.when(step > 0)
    def _():
        act_store.wait()
        gup_store.wait()

    for part in halves:
        hidden_low = hidden_ref[0, part, :]
        for at in range(0, units, chunk):
            span = pl.ds(at, chunk)
            upward = dot(hidden_low, up[:, span])
            cdf = 0.5 + 0.5 * lax.erf(upward * (0.5**0.5))
            density = jnp.exp(upward * upward * -0.5) * 0.3989422804014327
            act[part, span] = (upward * cdf).astype(bf16)
            gup[part, span] = (cdf + upward * density).astype(bf16)
    act_store.start()
    serve(1)
    sums2 = []
    for part in halves:
        z2, inv2 = norm_forward(held[part, :] + dot(act[part, :], down[...]))
        out_ref[0, part, :] = (z2 * gain2 + bias2).astype(bf16)
        dy = cot_ref[0, part, :].astype(f32)
        gsecond = norm_backward(dy * gain2, z2, inv2)
        sums2.append((jnp.sum(dy * z2, axis=0, keepdims=True), jnp.sum(dy, axis=0, keepdims=True)))
        gdown_ref[0, part, :] = gsecond.astype(bf16)
        held[part, :] = gsecond
    for part in halves:
        gdown = gdown_ref[0, part, :]
        for at in range(0, units, chunk):
            span = pl.ds(at, chunk)
            gact = dot_nt(gdown, down[span, :])
            gup[part, span] = (gact * gup[part, span].astype(f32)).astype(bf16)
    gup_store.start()
    serve(2)
    sums1 = []
    for part, inv1 in zip(halves, inverse1):
        ghidden = held[part, :] + dot_nt(gup[part, :], up[...])
        z1 = z_first[part, :]
        sums1.append((jnp.sum(ghidden * z1, axis=0, keepdims=True), jnp.sum(ghidden, axis=0, keepdims=True)))
        gatt_ref[0, part, :] = norm_backward(ghidden * gain1, z1, inv1).astype(bf16)
    for part in halves:
        go_ref[0, part, :] = (dot_nt(gatt_ref[0, part, :], wo[...]) * rinv_ref[part, :]).astype(bf16)
    output_grad[...] += dot_tn(mixed_ref[0], gatt_ref[0])
    for i, pieces in enumerate((sums1, sums2)):
        for j in range(2):
            sums_ref[2 * i + j : 2 * i + j + 1, :] += sum(piece[j] for piece in pieces)
    serve(3)

    @pl.when(step == last)
    def _():
        output_grad_ref[...] = output_grad[...].astype(bf16)
        e_store.wait()
        act_store.wait()
        gup_store.wait()
        q_store.wait()
        if line:
            for store in t_stores:
                store.wait()
            sums.finish()


def layer(set_kind, row_offset, compress, c, x, cot, weights, norms, line):
    sets, rows, width = x.shape
    longest, comp = compress.shape
    wq, wk, wv, wo, up, down = weights
    units = up.shape[1]
    tokens = per_set((rows, width))
    short = per_set((comp, width))
    anywhere = pl.BlockSpec(memory_space=pl.ANY)
    smem = pl.BlockSpec(memory_space=pltpu.SMEM)
    shape = lambda *dims, kind=bf16: jax.ShapeDtypeStruct(dims, kind)
    dma = lambda n: pltpu.SemaphoreType.DMA((n,))
    linked = []
    if line:
        count = sets * PIECES
        linked = [pltpu.VMEM((sets, rows, comp), bf16)]
        linked += [pltpu.VMEM((count, comp // PIECES, width), bf16)] * 3 + [dma(sets)] + [dma(count)] * 4
    more = dict(collective_id=0, has_side_effects=True) if line else {}
    return pl.pallas_call(
        functools.partial(layer_kernel, line),
        grid=(sets,),
        in_specs=[smem, smem, whole(compress.shape), anywhere if line else short, anywhere, tokens]
        + [whole((width,))] * 4
        + [anywhere] * 6,
        out_specs=[short] * 3 + [tokens] * 6 + [anywhere] * 5 + [whole((width, width)), whole((8, width))],
        out_shape=[shape(sets, comp, width)] * 3
        + [shape(sets, rows, width)] * 6
        + [shape(sets, rows, comp), shape(sets, rows, width)]
        + [shape(sets, rows, width // DH * comp)]
        + [shape(sets, rows, units)] * 2
        + [shape(width, width), shape(8, width, kind=f32)],
        scratch_shapes=[pltpu.VMEM(x.shape, bf16)] * 2
        + [pltpu.VMEM(w.shape, bf16) for w in weights]
        + [pltpu.VMEM((rows, width // DH * comp), bf16)]
        + [pltpu.VMEM((rows, units), bf16)] * 2
        + [pltpu.VMEM((rows, width), f32)] * 3
        + [pltpu.VMEM((width, width), f32), dma(6), dma(sets), dma(4)]
        + linked,
        compiler_params=params(**more),
        name="layer",
    )(set_kind, row_offset, compress, c, x, cot, *norms, *weights)


def pair_back(pair, e_ref, go_ref, mixed_ref, q_ref, kc_ref, vc_ref, gq_ref, gkt, gvt, half, minus):
    comp = kc_ref.shape[0]
    at = pair * LANES if isinstance(pair, int) else pl.multiple_of(pair * LANES, LANES)
    lanes = pl.ds(at, LANES)
    wide = pair * 2 * comp if isinstance(pair, int) else pl.multiple_of(pair * 2 * comp, LANES)
    e = e_ref[:, pl.ds(wide, 2 * comp)]
    keys = head_blocks(kc_ref[:, lanes], half)
    values = jnp.concatenate([head_blocks(vc_ref[:, lanes], half), minus], axis=1)
    go = go_ref[:, lanes]
    delta = (go.astype(f32) * mixed_ref[:, lanes].astype(f32)).astype(bf16)
    gp = dot_nt(jnp.concatenate([go, delta], axis=1), values)
    gs = (gp * e.astype(f32)).astype(bf16)
    gq_ref[:, lanes] = (dot(gs, keys) * SCALE).astype(bf16)
    for into, left, right in ((gkt, q_ref[:, lanes], gs), (gvt, go, e)):
        both = dot_tn(left, right)
        into[pl.ds(at, DH), :] = both[:DH, :comp].astype(bf16)
        into[pl.ds(at + DH, DH), :] = both[DH:, comp:].astype(bf16)


CHUNKS = 3
HERE = 1
BACK_PIECES = 4
BACK_LAG = 2


def back_kernel(
    line, long_ref, hidden_any, gup_any, act_any, gdown_any, output_any, e_any, go_any, mixed_any, q_any, kc_any, vc_any, wk_any, wv_any, x_any, c_any,
    gq_any, g_any, squares, output_out, up_out, down_out, up_rows, down_rows,
    hidden, gdown, feed, wk, wv, e, go, mixed, q, kc, vc, gq, gkt, gvt, gk, gv, own, from_left, from_right,
    up_part, down_part, output_part, load_sems, feed_sems, set_sems, out_sems, g_sem, late_sems, *scratch,
):
    scratch = list(scratch)
    take = lambda n: [scratch.pop(0) for _ in range(n)]
    sets, rows, width = q_any.shape
    comp = kc_any.shape[1]
    units = gup_any.shape[1]
    sums = LineSum(line, BACK_LAG, own, from_left, from_right, take(4))

    def copies(pairs, sems):
        return [pltpu.make_async_copy(src, dst, sems.at[i]) for i, (src, dst) in enumerate(pairs)]

    def feed_loads(chunk, which):
        if which == 0:
            wide, count, source = units // line, line, gup_any
        else:
            wide, count, source = units // 8, 8, act_any
        step = wide // CHUNKS
        return copies(
            [
                (source.at[:, pl.ds(pl.multiple_of(i * wide + chunk * step, LANES), step)], feed.at[which, :, pl.ds(i * step, step)])
                for i in range(count)
            ],
            feed_sems.at[which],
        )

    def set_loads(s):
        at = s % 2
        return copies(
            [(e_any.at[s], e.at[at]), (go_any.at[s], go.at[at]), (mixed_any.at[s], mixed.at[at]), (q_any.at[s], q.at[at]),
             (kc_any.at[s], kc.at[at]), (vc_any.at[s], vc.at[at])],
            set_sems.at[at],
        )

    def gq_store(s):
        return pltpu.make_async_copy(gq.at[s], gq_any.at[s], out_sems.at[s])

    def begin(some):
        for copy in some:
            copy.start()

    def end(some):
        for copy in some:
            copy.wait()

    weights = copies(((output_any, output_part), (hidden_any, hidden), (gdown_any, gdown), (wk_any, wk), (wv_any, wv)), load_sems)
    begin(weights[:1])
    begin(set_loads(0))
    begin(weights[3:])
    near = Neighbours(line)
    greet(near.everyone())
    sums.prepare()

    jobs = {"o": (Scatter(True, output_part, *take(5)), LineScatter(*take(5)), output_out)}
    lines = [LineScatter(*take(5)), LineScatter(*take(5))]
    kept = (take(5), take(5))

    def scatter_job(which, chunk):
        buffers = [ref.at[chunk] for ref in kept[which]]
        return Scatter(which == 0, (up_part, down_part)[which], *buffers)

    for chunk in range(CHUNKS):
        for which in range(2):
            if chunk < HERE:
                jobs[which, chunk] = (scatter_job(which, chunk), lines[which], (up_out, down_out)[which])
            else:
                jobs[which, chunk] = (scatter_job(which, chunk), None, (up_rows, down_rows)[which].at[chunk - HERE])

    def across(name):
        job, line_job, _ = jobs[name]
        line_scatter_blocks(line_job.blocks, job.done(), line)
        line_job.start()

    def feed_grad(which):
        if which == 0:
            up_part[...] = dot_tn(hidden[...], feed[0]).astype(bf16).reshape(up_part.shape)
        else:
            down_part[...] = dot_tn(feed[1], gdown[...]).astype(bf16).reshape(down_part.shape)

    half = lax.broadcasted_iota(jnp.int32, (comp, LANES), 1) < DH
    minus = head_blocks(jnp.full((comp, LANES), -1.0, bf16), half)

    def heads(s, pairs):
        at = s % 2
        for pair in pairs:
            pair_back(pair, e.at[at], go.at[at], mixed.at[at], q.at[at], kc.at[at], vc.at[at], gq.at[s], gkt, gvt, half, minus)

    def joins(s):
        g = dot(wk[...], gkt[...]) + dot(wv[...], gvt[...])
        own[pl.ds(s * BACK_PIECES, BACK_PIECES)] = g.astype(bf16).reshape(BACK_PIECES, width // BACK_PIECES, comp)
        gk[s] = gkt[...].T
        gv[s] = gvt[...].T
        gq_store(s).start()

    o, (u0, u1, u2), (d0, d1) = jobs["o"][0], [jobs[0, i][0] for i in range(3)], [jobs[1, i][0] for i in range(2)]
    weights[0].wait()
    o.start()

    def steps(s, by_set):
        for at, due in by_set.items():

            @pl.when(s == at)
            def _():
                for one in due:
                    one()

    def work(s, carry):
        end(set_loads(s))
        steps(s, {
            0: [lambda: begin(weights[1:2]), lambda: begin(feed_loads(0, 0))],
            1: [lambda: begin(feed_loads(1, 0)), lambda: begin(weights[2:3]), lambda: begin(feed_loads(0, 1))],
            2: [lambda: begin(feed_loads(1, 1)), lambda: begin(set_loads(3))],
            3: [lambda: begin(feed_loads(2, 0)), lambda: begin(feed_loads(2, 1))],
        })
        pairs = width // LANES // 2

        def some_heads(half_at, carry):
            heads(s, [half_at * pairs + i for i in range(pairs)])

            @pl.when(half_at == 0)
            def _():
                steps(s, {0: [o.first], 1: [u0.first], 2: [d0.first], 3: [d1.first]})

            return carry

        lax.fori_loop(0, 2, some_heads, 0)
        steps(s, {0: [lambda: end(weights[3:])], 1: [o.second], 2: [u0.second], 3: [u1.second, d0.second]})
        joins(s)
        sums.serve_many(s * BACK_PIECES, 2)

        @pl.when(s != 2)
        def _():
            chunk = s - s // 3
            end(feed_loads(chunk, 0))
            steps(s, {0: [lambda: end(weights[1:2]), lambda: begin(set_loads(1))], 1: [lambda: begin(set_loads(2))]})
            feed_grad(0)
            scatter_job(0, chunk).start()
            sums.serve_many(s * BACK_PIECES + 2, 2)

        @pl.when(s > 0)
        def _():
            end(feed_loads(s - 1, 1))
            steps(s, {1: [lambda: end(weights[2:3])]})
            feed_grad(1)

            @pl.when(s < sets - 1)
            def _():
                scatter_job(1, s - 1).start()

        steps(s, {1: [u1.first], 2: [lambda: sums.serve_many(2 * BACK_PIECES + 2, 2)], 3: [begin_late, u2.first]})
        return carry

    late = copies(((x_any, hidden), (c_any, gdown.at[: c_any.shape[0]])), late_sems)

    def begin_late():
        begin(late)

    lax.fori_loop(0, sets, work, 0)
    d2 = jobs[1, 2][0]
    d2.start()
    places = (feed.at[0, :width, :width], feed.at[0, width : 2 * width, :width], feed.at[1, :width, :width])
    flat = lambda ref, span: ref[:, :, span].reshape(-1, span.size)
    sources = ((hidden, gq), (gdown.at[: c_any.shape[0]], gk), (gdown.at[: c_any.shape[0]], gv))
    square_stores = [pltpu.make_async_copy(places[i], squares.at[i], late_sems.at[2 + i]) for i in range(3)]

    def square_grad_part(i):
        left, right = sources[i]
        grad_columns(places[i], lambda: left[...], lambda span: flat(right, span))
        square_stores[i].start()

    served = sets * BACK_PIECES
    sums.serve_many(served, 2)
    late[0].wait()
    square_grad_part(0)
    d2.first()
    d1.second()
    sums.serve_many(served + 2, 1)
    late[1].wait()
    square_grad_part(1)
    sums.serve_many(served + 3, 1)
    square_grad_part(2)
    sums.serve_many(served + 4, 1)
    u2.second()
    sums.serve_many(served + 5, sums.slots() - served - 5)
    d2.second()
    for name in ("o", (0, 0), (1, 0)):
        across(name)
    for s in range(sets):
        for piece in range(s * BACK_PIECES, (s + 1) * BACK_PIECES):
            own[piece] = sums.total(piece, long_ref[s] > 0)
    g_store = pltpu.make_async_copy(own, g_any, g_sem.at[0])
    g_store.start()
    for name in ("o", (0, 0), (1, 0)):
        jobs[name][1].middle()
    for name in jobs:
        job, line_job, out = jobs[name]
        if line_job is not None:
            unfold(line_job.done(), out)
        else:
            out[...] = job.done().astype(bf16)
    for name in jobs:
        job, line_job, _ = jobs[name]
        job.finish()
        if line_job is not None:
            line_job.finish()
    for store in square_stores:
        store.wait()
    for s in range(sets):
        gq_store(s).wait()
    g_store.wait()
    sums.finish()


def back(set_kind, hidden, gup, act, gdown, output_part, e, go, mixed, q, kc, vc, wk, wv, x, c):
    line = lax.axis_size("seq")
    sets, rows, width = q.shape
    comp = kc.shape[1]
    tokens, units = gup.shape
    eighth = width // 8
    wide, tall = units // CHUNKS, units // 8 // CHUNKS
    count = sets * BACK_PIECES
    dma = lambda *n: pltpu.SemaphoreType.DMA(n)
    vmem, anywhere = pl.BlockSpec(memory_space=pltpu.VMEM), pl.BlockSpec(memory_space=pl.ANY)
    shape = lambda *dims, kind=bf16: jax.ShapeDtypeStruct(dims, kind)
    buffer = lambda *dims, kind=bf16: pltpu.VMEM(dims, kind)
    scratch = [buffer(tokens, width)] * 2 + [buffer(2, tokens, wide)] + [buffer(width, width)] * 2
    scratch += [buffer(2, rows, e.shape[2])] + [buffer(2, rows, width)] * 3 + [buffer(2, comp, width)] * 2
    scratch += [buffer(sets, rows, width)] + [buffer(width, comp)] * 2 + [buffer(sets, comp, width)] * 2
    scratch += [buffer(count, width // BACK_PIECES, comp)] * 3
    scratch += [buffer(2, 2, 2, eighth, wide), buffer(2, 2, 2, tall, width), buffer(2, 2, 2, eighth, width)]
    scratch += [dma(5), dma(2, 8), dma(2, 6), dma(sets), dma(1), dma(5)] + [dma(count)] * 4
    scratch += scatter_scratch(eighth, width)
    for size in ((eighth, width), (eighth, wide), (tall, width)):
        scratch += line_scratch(*size, line)
    scratch += scatter_scratch(eighth, wide, CHUNKS) + scatter_scratch(tall, width, CHUNKS)
    return pl.pallas_call(
        functools.partial(back_kernel, line),
        in_specs=[pl.BlockSpec(memory_space=pltpu.SMEM)] + [anywhere] * 15,
        out_specs=[anywhere] * 3 + [vmem] * 5,
        out_shape=[
            shape(sets, rows, width),
            shape(count, width // BACK_PIECES, comp),
            shape(3, width, width),
            shape(eighth, width // line, kind=f32),
            shape(eighth, wide // line * HERE, kind=f32), shape(tall * HERE, width // line, kind=f32),
            shape(CHUNKS - HERE, eighth, wide), shape(CHUNKS - HERE, tall, width),
        ],
        scratch_shapes=scratch,
        compiler_params=params(collective_id=1, has_side_effects=True),
        name="back",
    )(set_kind, hidden, gup, act, gdown, output_part.reshape(2, 2, 2, eighth, width), e, go, mixed, q, kc, vc, wk, wv, x, c)


def attention_back_kernel(
    e_ref, go_ref, mixed_ref, q_ref, kc_ref, vc_ref, wk_ref, wv_ref,
    gq_ref, gk_ref, gv_ref, g_ref,
    gkt, gvt,
):
    width = q_ref.shape[2]
    comp = kc_ref.shape[1]
    half = lax.broadcasted_iota(jnp.int32, (comp, LANES), 1) < DH
    minus = head_blocks(jnp.full((comp, LANES), -1.0, bf16), half)
    refs = [ref.at[0] for ref in (e_ref, go_ref, mixed_ref, q_ref, kc_ref, vc_ref, gq_ref)]
    for pair in range(width // LANES):
        pair_back(pair, *refs, gkt, gvt, half, minus)
    g_ref[0] = (dot(wk_ref[...], gkt[...]) + dot(wv_ref[...], gvt[...])).astype(bf16)
    gk_ref[0] = gkt[...].T
    gv_ref[0] = gvt[...].T


def attention_back(e, go, mixed, q, kc, vc, wk, wv):
    sets, rows, width = q.shape
    comp = kc.shape[1]
    outs = [
        ((rows, width), bf16),
        ((comp, width), bf16),
        ((comp, width), bf16),
        ((width, comp), bf16),
    ]
    tokens = per_set((rows, width))
    short = per_set((comp, width))
    return pl.pallas_call(
        attention_back_kernel,
        grid=(sets,),
        in_specs=[per_set(e.shape[1:])] + [tokens] * 3 + [short] * 2
        + [whole(w.shape) for w in (wk, wv)],
        out_specs=[per_set(shape) for shape, _ in outs],
        out_shape=[jax.ShapeDtypeStruct((sets,) + shape, kind) for shape, kind in outs],
        scratch_shapes=[pltpu.VMEM((width, comp), bf16)] * 2,
        compiler_params=params(),
        name="attention_back",
    )(e, go, mixed, q, kc, vc, wk, wv)


def feed_grads_kernel(hidden_ref, gup_ref, act_ref, gdown_ref, up_out, down_out):
    up_out[...] = dot_tn(hidden_ref[...], gup_ref[...]).astype(bf16)
    down_out[...] = dot_tn(act_ref[...], gdown_ref[...]).astype(bf16)


def feed_grads(hidden, gup, act, gdown):
    tokens, width = hidden.shape
    units = gup.shape[1]
    chunk = 512
    return pl.pallas_call(
        feed_grads_kernel,
        grid=(units // chunk,),
        in_specs=[
            whole((tokens, width)),
            pl.BlockSpec((tokens, chunk), lambda i: (0, i)),
            pl.BlockSpec((tokens, chunk), lambda i: (0, i)),
            whole((tokens, width)),
        ],
        out_specs=[
            pl.BlockSpec((width, chunk), lambda i: (0, i)),
            pl.BlockSpec((chunk, width), lambda i: (i, 0)),
        ],
        out_shape=[jax.ShapeDtypeStruct((width, units), bf16), jax.ShapeDtypeStruct((units, width), bf16)],
        compiler_params=params(),
        name="feed_grads",
    )(hidden, gup, act, gdown)


def square_grad_kernel(left_ref, right_ref, out_ref):
    out_ref[...] = dot_tn(left_ref[...], right_ref[...]).astype(bf16)


def square_grad(left, right):
    count, width = left.shape
    return pl.pallas_call(
        square_grad_kernel,
        grid=(1,),
        in_specs=[whole((count, width)), whole((count, width))],
        out_specs=whole((width, width)),
        out_shape=jax.ShapeDtypeStruct((width, width), bf16),
        compiler_params=params(),
        name="square_grad",
    )(left, right)


def last_kernel(kind_ref, offset_ref, table_any, x_any, g_any, gfirst_any, gq_any, wq_any, out_any, compress_ref,
                table, x, g, gfirst, gq, wq, out, total, load_sems, weight_sem, out_sems):
    sets, rows, _ = x.shape
    longest = compress_ref.shape[0]
    pairs = ((g_any, g), (x_any, x), (gq_any, gq), (table_any, table), (gfirst_any, gfirst))
    loads = [[pltpu.make_async_copy(src.at[s], dst.at[s], load_sems.at[s, i]) for i, (src, dst) in enumerate(pairs)] for s in range(sets)]
    stores = [pltpu.make_async_copy(out.at[s], out_any.at[s], out_sems.at[s]) for s in range(sets)]
    weight = pltpu.make_async_copy(wq_any, wq, weight_sem.at[0])
    for load in loads[0]:
        load.start()
    weight.start()
    for s in range(1, sets):
        for load in loads[s]:
            load.start()
    total[...] = jnp.zeros_like(total)
    weight.wait()

    def work(s, carry):
        for i, (src, dst) in enumerate(pairs):
            pltpu.make_async_copy(src.at[s], dst.at[s], load_sems.at[s, i]).wait()
        out[s] = gfirst[s].astype(f32) + (dot_nt(table[s], g[s]) + dot_nt(gq[s], wq[...]))
        pltpu.make_async_copy(out.at[s], out_any.at[s], out_sems.at[s]).start()
        terms = dot(x[s], g[s])
        begin, shift = aligned(own_start(kind_ref, offset_ref, s, rows, longest // 4))
        padded = jnp.concatenate([terms, jnp.zeros((TILE, terms.shape[1]), f32)], axis=0)
        total[pl.ds(begin, rows + TILE), :] += pltpu.roll(padded, shift, 0)
        return carry

    lax.fori_loop(0, sets, work, 0)
    compress_ref[...] = total[:longest, :].astype(compress_ref.dtype)
    for store in stores:
        store.wait()


def last(kinds, offsets, table, x, g, gfirst, gq, wq, longest, kind):
    sets, rows, width = x.shape
    comp = table.shape[2]
    anywhere, smem = pl.BlockSpec(memory_space=pl.ANY), pl.BlockSpec(memory_space=pltpu.SMEM)
    dma = lambda *n: pltpu.SemaphoreType.DMA(n)
    return pl.pallas_call(
        last_kernel,
        in_specs=[smem] * 2 + [anywhere] * 6,
        out_specs=[anywhere, pl.BlockSpec(memory_space=pltpu.VMEM)],
        out_shape=[
            jax.ShapeDtypeStruct((sets, rows, width), f32),
            jax.ShapeDtypeStruct((longest, comp), kind),
        ],
        scratch_shapes=[pltpu.VMEM(v.shape, v.dtype) for v in (table, x, g, gfirst, gq, wq)]
        + [pltpu.VMEM(x.shape, f32), pltpu.VMEM((longest + TILE, comp), f32), dma(sets, 5), dma(1), dma(sets)],
        compiler_params=params(),
        name="last",
    )(kinds, offsets, table, x, g, gfirst, gq, wq)


def finish_kernel(layer_any, table, norms, up_first, up_more, down_first, down_more, *refs):
    (squares, output), (layer_out, table_out, up_out, down_out), outs, (held, sems) = refs[:2], refs[2:6], refs[6:-2], refs[-2:]
    sets = range(held.shape[0])
    loads = [pltpu.make_async_copy(layer_any.at[i], held.at[i], sems.at[0, i]) for i in sets]
    stores = [pltpu.make_async_copy(held.at[i], layer_out.at[i], sems.at[1, i]) for i in sets]
    for load in loads:
        load.start()
    for load, store in zip(loads, stores):
        load.wait()
        store.start()
    table_out[...] = table[...].astype(f32).reshape(table_out.shape)
    wide, tall = up_first.shape[1], down_first.shape[0]
    up_out[:, :wide] = up_first[...]
    down_out[:, :tall] = down_first[...].T
    for i in range(up_more.shape[0]):
        up_out[:, (i + 1) * wide : (i + 2) * wide] = up_more[i]
    for i in range(down_more.shape[0]):
        down_out[:, (i + 1) * tall : (i + 2) * tall] = down_more[i].T
    for i in range(4):
        outs[i][...] = squares[i] if i < 3 else output[...]
        outs[4 + i][...] = norms[i, :]
    for store in stores:
        store.wait()


def finish(layer_out, table, norms, up_first, up_more, down_first, down_more, squares, output):
    vmem, anywhere = pl.BlockSpec(memory_space=pltpu.VMEM), pl.BlockSpec(memory_space=pl.ANY)
    width = norms.shape[1]
    out = lambda *dims: jax.ShapeDtypeStruct(dims, f32)
    return pl.pallas_call(
        finish_kernel,
        in_specs=[anywhere] + [vmem] * 8,
        out_specs=[anywhere] + [vmem] * 11,
        out_shape=[
            jax.ShapeDtypeStruct(layer_out.shape, layer_out.dtype),
            out(table.size // table.shape[-1], table.shape[-1]),
            out(up_first.shape[0], up_first.shape[1] * (1 + up_more.shape[0])),
            out(down_first.shape[1], down_first.shape[0] * (1 + down_more.shape[0])),
        ]
        + [out(*output.shape)] * 4
        + [out(width)] * 4,
        scratch_shapes=[pltpu.VMEM(layer_out.shape, layer_out.dtype), pltpu.SemaphoreType.DMA((2, layer_out.shape[0]))],
        compiler_params=params(),
        name="finish",
    )(layer_out, table, norms, up_first, up_more, down_first, down_more, squares, output)


def sequence_sum(part, is_long, row_count, shortest):
    seq_count = lax.axis_size("seq")
    total = lax.psum(part, "seq")
    span = shortest // row_count
    if span > 1:
        groups = [list(range(i, i + span)) for i in range(0, seq_count, span)]
        part = lax.psum(part, "seq", axis_index_groups=groups)
    return jnp.where(is_long[:, None, None], total, part)


def table_start(set_kind, row_offset, block_index, row_count, shortest):
    position = block_index * row_count
    member = position // shortest
    chosen = jnp.sum(jnp.where(jnp.arange(4)[None, :] == member, row_offset, 0), axis=1)
    return jnp.where(set_kind > 0, position, chosen + position % shortest)


def local(
    inputs, cotangent, set_kind, row_offset, query_w, key_w, value_w, output_w, up_w, down_w, compress,
    first_gain, first_bias, second_gain, second_bias,
):
    sets, rows, width = inputs.shape
    longest, comp = compress.shape
    shortest = longest // 4
    ranked = lax.axis_index("seq")
    tokens = sets * rows
    is_long = set_kind > 0
    norms = (first_gain, first_bias, second_gain, second_bias)
    linked = lax.axis_size("batch") == 8 and lax.axis_size("seq") == 4 and rows == shortest
    weights = (query_w, key_w, value_w, output_w, up_w, down_w)
    if linked:
        summed, line = inputs, lax.axis_size("seq")
    else:
        starts = table_start(set_kind, row_offset, ranked, rows, shortest).astype(jnp.int32)
        table, part, _ = front(starts, compress, inputs, query_w)
        summed, line = sequence_sum(part, is_long, rows, shortest), 0
    (kc, vc, summed, mixed, hidden, layer_out, gdown, gatt, go, new_table, queries, e, act, gup, output_part, norm_sums) = layer(
        set_kind, row_offset, compress, summed, inputs, cotangent, weights, norms, line
    )
    flat = lambda v: v.reshape(-1, v.shape[-1])
    if linked:
        gq, g, squares, output_grad, up_first, down_first, up_rows, down_rows = back(
            set_kind, flat(hidden), flat(gup), flat(act), flat(gdown), output_part, e, go, mixed, queries, kc, vc, key_w, value_w,
            flat(inputs), flat(summed),
        )
        g = g.reshape(sets, width, comp)
        input_grad, compress_part = last(set_kind, row_offset, new_table, inputs, g, gatt, gq, query_w, longest, bf16)
        table_sum, norm_total, up_more, down_more, squares = closing(
            compress_part, norm_sums, up_rows, down_rows, squares
        )
        layer_out, compress_grad, up_grad, down_grad, *rest = finish(
            layer_out, table_sum, norm_total, up_first, up_more, down_first, down_more, squares, output_grad
        )
        weights, norm_grads = tuple(rest[:4]) + (up_grad, down_grad.T), rest[4:]
    else:
        up_part, down_part = feed_grads(flat(hidden), flat(gup), flat(act), flat(gdown))
        gq, gk, gv, g_part = attention_back(e, go, mixed, queries, kc, vc, key_w, value_w)
        g = sequence_sum(g_part, is_long, rows, shortest)
        query_part = square_grad(flat(inputs), flat(gq))
        key_part = square_grad(flat(summed), flat(gk))
        value_part = square_grad(flat(summed), flat(gv))
        input_grad, compress_part = last(set_kind, row_offset, table, inputs, g, gatt, gq, query_w, longest, f32)

        def scattered(v):
            v = lax.psum_scatter(v, "seq", scatter_dimension=1, tiled=True)
            return lax.psum_scatter(v, "batch", scatter_dimension=0, tiled=True).astype(f32)

        parts = (query_part, key_part, value_part, output_part, up_part, down_part)
        weights = tuple(scattered(v) for v in parts)
        compress_grad, norm_grads = lax.psum((compress_part, norm_sums), ("batch", "seq"))
    return (layer_out, input_grad) + weights + (compress_grad,) + tuple(norm_grads[i] for i in range(4))


def solution(mesh):
    tokens = P("batch", "seq", None)
    in_specs = (tokens, tokens, P("batch"), P("batch", None)) + (P(),) * 11
    out_specs = (tokens, tokens) + (P("batch", "seq"),) * 6 + (P(),) * 5
    return jax.shard_map(local, mesh=mesh, in_specs=in_specs, out_specs=out_specs, check_vma=False)
```

profile of v0, /device:TPU:0, one launch (start us, length us, event | category | flops | bytes accessed | tf_op | source)
XLA Modules:
  0.0 255.9 jit_solution(16866906354173027386)
XLA Ops:
  0.6 108.1 %layer.1 = (bf16[4,256,768]{2,1,0:T(8,128)(2,1)}, bf16[4,256,768]{2,1,0:T(8,128)(2,1)}, bf16[4,256,768]{2,1,0:T(8,128)(2,1)}, bf16[4,512,768]{2,1,0:T(8,128)(2,1...) custom-call(s32[4]{0:T(128)} %kind_ref.1, ...), custom_call_target="tpu_custom_call" | custom-call | tf_op jit(solution)/shard_map/layer/pallas_call | solution.py:735
  108.8 81.7 %back.1 = (bf16[4,512,768]{2,1,0:T(8,128)(2,1)}, bf16[16,192,256]{2,1,0:T(8,128)(2,1)}, bf16[3,768,768]{2,1,0:T(8,128)(2,1)}, f32[96,192]{1,0:T(8,128)}, f32[96,...) custom-call(s32[4]{0:T(128)} %kind_ref.1, ...), custom_call_target="tpu_custom_call" | custom-call | tf_op jit(solution)/shard_map/back/pallas_call | solution.py:1024
  190.5 12.9 %last.1 = (f32[4,512,768]{2,1,0:T(8,128)}, bf16[2048,256]{1,0:T(8,128)(2,1)}) custom-call(s32[4]{0:T(128)} %kind_ref.1, s32[4,4]{1,0:T(4,128)} %offset_ref.3, bf16[4,512,256]{2,1,0:T(8,128)(2,1)} %get-tuple-element.57.table_any, bf16[4,512,768]{2,1,0:T(8,128)(2,1)} %x_any.3, bf16[4,768,256]{2,1,0:T(8,128)(2,1)} %bitcast.17, ...), custom_call_target="tpu_custom_call" | custom-call | tf_op jit(solution)/shard_map/last/pallas_call | solution.py:1167
  203.5 46.2 %closing.1 = (bf16[2,4,4,64,256]{4,3,2,1,0:T(8,128)(2,1)}, f32[8,768]{1,0:T(8,128)}, f32[2,96,256]{2,1,0:T(8,128)}, f32[2,128,192]{2,1,0:T(8,128)}, f32[3,96,192]{2,1,0:T(8,128)}) custom-call(bf16[2,4,4,64,256]{4,3,2,1,0:T(8,128)(2,1)} %bitcast.20, f32[8,768]{1,0:T(8,128)} %get-tuple-element.74.norms_ref, bf16[2,96,1024]{2,1,0:T(8,128)(2,1)} %get-tuple-element.75.up_ref, ...), custom_call_target="tpu_custom_call" | custom-call | tf_op jit(solution)/shard_map/closing/pallas_call | solution.py:424
  249.7 6.1 %finish.1 = (bf16[4,512,768]{2,1,0:T(8,128)(2,1)}, f32[2048,256]{1,0:T(8,128)}, f32[96,768]{1,0:T(8,128)}, f32[192,384]{1,0:T(8,128)}, f32[96,192]{1,0:T(8,128)}...) custom-call(bf16[4,512,768]{2,1,0:T(8,128)(2,1)} %get-tuple-element., ...), custom_call_target="tpu_custom_call" | custom-call | tf_op jit(solution)/shard_map/finish/pallas_call | solution.py:1211
where the time goes:
time: 256 us
  Pallas kernels  255 us (100%)
    pallas_call x1, Pallas kernels, layer(): pl.pallas_call(functools.partial(layer_kernel, line), grid=(sets,), in_sp...  108 us
    pallas_call x1, Pallas kernels, back(): pl.pallas_call(functools.partial(back_kernel, line), in_specs=[pl.BlockSp...  81.7 us
    pallas_call x1, Pallas kernels, closing(): pl.pallas_call(functools.partial(closing_kernel, line), in_specs=[vmem] *...  46.2 us
    pallas_call x1, Pallas kernels, last(): pl.pallas_call(last_kernel, in_specs=[smem] * 2 + [anywhere] * 6, out_spe...  12.9 us
    pallas_call x1, Pallas kernels, finish(): pl.pallas_call(finish_kernel, in_specs=[anywhere] + [vmem] * 8, out_specs...  6.08 us

commit v1 on v0

--- a/solution.py
+++ b/solution.py
@@ -386,12 +386,12 @@
         job.middle()
     total.advance()
     query.second()
+    key.second()
     total.advance()
-    key.second()
     for job, out in across:
         unfold(job.done(), out)
+    value.second()
     total.advance()
-    value.second()
     jobs = [(job, square_lines[i], square_out.at[i]) for i, job in enumerate((query, key, value))]
     for job, line_job, _ in jobs:
         line_scatter_blocks(line_job.blocks, job.done(), line)

time: 256 us -> 255 us (level)
  no operation moved by 1% of the time
where the time goes in v1:
time: 255 us; the launch traced here: 254 us
  Pallas kernels  253 us (99%)
    pallas_call x1, Pallas kernels, layer(): pl.pallas_call(functools.partial(layer_kernel, line), grid=(sets,), in_sp...  108 us
    pallas_call x1, Pallas kernels, back(): pl.pallas_call(functools.partial(back_kernel, line), in_specs=[pl.BlockSp...  81.7 us
    pallas_call x1, Pallas kernels, closing(): pl.pallas_call(functools.partial(closing_kernel, line), in_specs=[vmem] *...  44.6 us
    pallas_call x1, Pallas kernels, last(): pl.pallas_call(last_kernel, in_specs=[smem] * 2 + [anywhere] * 6, out_spe...  12.9 us
    pallas_call x1, Pallas kernels, finish(): pl.pallas_call(finish_kernel, in_specs=[anywhere] + [vmem] * 8, out_specs...  6.08 us

profile of v1, /device:TPU:0, one launch (start us, length us, event | category | flops | bytes accessed | tf_op | source)
XLA Modules:
  0.0 254.3 jit_solution(3841833082864435036)
XLA Ops:
  0.6 108.1 %layer.1 = (bf16[4,256,768]{2,1,0:T(8,128)(2,1)}, bf16[4,256,768]{2,1,0:T(8,128)(2,1)}, bf16[4,256,768]{2,1,0:T(8,128)(2,1)}, bf16[4,512,768]{2,1,0:T(8,128)(2,1...) custom-call(s32[4]{0:T(128)} %kind_ref.1, ...), custom_call_target="tpu_custom_call" | custom-call | tf_op jit(solution)/shard_map/layer/pallas_call | solution.py:735
  108.8 81.7 %back.1 = (bf16[4,512,768]{2,1,0:T(8,128)(2,1)}, bf16[16,192,256]{2,1,0:T(8,128)(2,1)}, bf16[3,768,768]{2,1,0:T(8,128)(2,1)}, f32[96,192]{1,0:T(8,128)}, f32[96,...) custom-call(s32[4]{0:T(128)} %kind_ref.1, ...), custom_call_target="tpu_custom_call" | custom-call | tf_op jit(solution)/shard_map/back/pallas_call | solution.py:1024
  190.5 12.9 %last.1 = (f32[4,512,768]{2,1,0:T(8,128)}, bf16[2048,256]{1,0:T(8,128)(2,1)}) custom-call(s32[4]{0:T(128)} %kind_ref.1, s32[4,4]{1,0:T(4,128)} %offset_ref.3, bf16[4,512,256]{2,1,0:T(8,128)(2,1)} %get-tuple-element.57.table_any, bf16[4,512,768]{2,1,0:T(8,128)(2,1)} %x_any.3, bf16[4,768,256]{2,1,0:T(8,128)(2,1)} %bitcast.17, ...), custom_call_target="tpu_custom_call" | custom-call | tf_op jit(solution)/shard_map/last/pallas_call | solution.py:1167
  203.5 44.6 %closing.1 = (bf16[2,4,4,64,256]{4,3,2,1,0:T(8,128)(2,1)}, f32[8,768]{1,0:T(8,128)}, f32[2,96,256]{2,1,0:T(8,128)}, f32[2,128,192]{2,1,0:T(8,128)}, f32[3,96,192]{2,1,0:T(8,128)}) custom-call(bf16[2,4,4,64,256]{4,3,2,1,0:T(8,128)(2,1)} %bitcast.20, f32[8,768]{1,0:T(8,128)} %get-tuple-element.74.norms_ref, bf16[2,96,1024]{2,1,0:T(8,128)(2,1)} %get-tuple-element.75.up_ref, ...), custom_call_target="tpu_custom_call" | custom-call | tf_op jit(solution)/shard_map/closing/pallas_call | solution.py:424
  248.1 6.1 %finish.1 = (bf16[4,512,768]{2,1,0:T(8,128)(2,1)}, f32[2048,256]{1,0:T(8,128)}, f32[96,768]{1,0:T(8,128)}, f32[192,384]{1,0:T(8,128)}, f32[96,192]{1,0:T(8,128)}...) custom-call(bf16[4,512,768]{2,1,0:T(8,128)(2,1)} %get-tuple-element., ...), custom_call_target="tpu_custom_call" | custom-call | tf_op jit(solution)/shard_map/finish/pallas_call | solution.py:1211

commit v2 on v1

--- a/solution.py
+++ b/solution.py
@@ -588,7 +588,7 @@
 
     def serve(part):
         if line:
-            count = PIECES // 4
+            count = PIECES // 2
 
             @pl.when(step < last)
             def _():
@@ -640,7 +640,6 @@
     lax.fori_loop(0, 2, some_heads, 0)
     e_store.start()
     first_use(loads[3])
-    serve(0)
     gain1, bias1, gain2, bias2 = (ref[...].reshape(1, width) for ref in (gain1_ref, bias1_ref, gain2_ref, bias2_ref))
     size = rows // HALVES
     halves = [pl.ds(h * size, size) for h in range(HALVES)]
@@ -670,7 +669,7 @@
             act[part, span] = (upward * cdf).astype(bf16)
             gup[part, span] = (cdf + upward * density).astype(bf16)
     act_store.start()
-    serve(1)
+    serve(0)
     sums2 = []
     for part in halves:
         z2, inv2 = norm_forward(held[part, :] + dot(act[part, :], down[...]))
@@ -687,7 +686,6 @@
             gact = dot_nt(gdown, down[span, :])
             gup[part, span] = (gact * gup[part, span].astype(f32)).astype(bf16)
     gup_store.start()
-    serve(2)
     sums1 = []
     for part, inv1 in zip(halves, inverse1):
         ghidden = held[part, :] + dot_nt(gup[part, :], up[...])
@@ -700,7 +698,7 @@
     for i, pieces in enumerate((sums1, sums2)):
         for j in range(2):
             sums_ref[2 * i + j : 2 * i + j + 1, :] += sum(piece[j] for piece in pieces)
-    serve(3)
+    serve(1)
 
     @pl.when(step == last)
     def _():

time: 255 us -> 254 us (level)
  no operation moved by 1% of the time
where the time goes in v2:
time: 254 us
  Pallas kernels  253 us (100%)
    pallas_call x1, Pallas kernels, layer(): pl.pallas_call(functools.partial(layer_kernel, line), grid=(sets,), in_sp...  108 us
    pallas_call x1, Pallas kernels, back(): pl.pallas_call(functools.partial(back_kernel, line), in_specs=[pl.BlockSp...  81.7 us
    pallas_call x1, Pallas kernels, closing(): pl.pallas_call(functools.partial(closing_kernel, line), in_specs=[vmem] *...  44.6 us
    pallas_call x1, Pallas kernels, last(): pl.pallas_call(last_kernel, in_specs=[smem] * 2 + [anywhere] * 6, out_spe...  12.9 us
    pallas_call x1, Pallas kernels, finish(): pl.pallas_call(finish_kernel, in_specs=[anywhere] + [vmem] * 8, out_specs...  6.08 us

profile of v2, /device:TPU:0, one launch (start us, length us, event | category | flops | bytes accessed | tf_op | source)
XLA Modules:
  0.0 253.9 jit_solution(11694429832112668898)
XLA Ops:
  0.6 107.7 %layer.1 = (bf16[4,256,768]{2,1,0:T(8,128)(2,1)}, bf16[4,256,768]{2,1,0:T(8,128)(2,1)}, bf16[4,256,768]{2,1,0:T(8,128)(2,1)}, bf16[4,512,768]{2,1,0:T(8,128)(2,1...) custom-call(s32[4]{0:T(128)} %kind_ref.1, ...), custom_call_target="tpu_custom_call" | custom-call | tf_op jit(solution)/shard_map/layer/pallas_call | solution.py:733
  108.4 81.7 %back.1 = (bf16[4,512,768]{2,1,0:T(8,128)(2,1)}, bf16[16,192,256]{2,1,0:T(8,128)(2,1)}, bf16[3,768,768]{2,1,0:T(8,128)(2,1)}, f32[96,192]{1,0:T(8,128)}, f32[96,...) custom-call(s32[4]{0:T(128)} %kind_ref.1, ...), custom_call_target="tpu_custom_call" | custom-call | tf_op jit(solution)/shard_map/back/pallas_call | solution.py:1022
  190.1 12.9 %last.1 = (f32[4,512,768]{2,1,0:T(8,128)}, bf16[2048,256]{1,0:T(8,128)(2,1)}) custom-call(s32[4]{0:T(128)} %kind_ref.1, s32[4,4]{1,0:T(4,128)} %offset_ref.3, bf16[4,512,256]{2,1,0:T(8,128)(2,1)} %get-tuple-element.57.table_any, bf16[4,512,768]{2,1,0:T(8,128)(2,1)} %x_any.3, bf16[4,768,256]{2,1,0:T(8,128)(2,1)} %bitcast.17, ...), custom_call_target="tpu_custom_call" | custom-call | tf_op jit(solution)/shard_map/last/pallas_call | solution.py:1165
  203.0 44.6 %closing.1 = (bf16[2,4,4,64,256]{4,3,2,1,0:T(8,128)(2,1)}, f32[8,768]{1,0:T(8,128)}, f32[2,96,256]{2,1,0:T(8,128)}, f32[2,128,192]{2,1,0:T(8,128)}, f32[3,96,192]{2,1,0:T(8,128)}) custom-call(bf16[2,4,4,64,256]{4,3,2,1,0:T(8,128)(2,1)} %bitcast.20, f32[8,768]{1,0:T(8,128)} %get-tuple-element.74.norms_ref, bf16[2,96,1024]{2,1,0:T(8,128)(2,1)} %get-tuple-element.75.up_ref, ...), custom_call_target="tpu_custom_call" | custom-call | tf_op jit(solution)/shard_map/closing/pallas_call | solution.py:424
  247.6 6.1 %finish.1 = (bf16[4,512,768]{2,1,0:T(8,128)(2,1)}, f32[2048,256]{1,0:T(8,128)}, f32[96,768]{1,0:T(8,128)}, f32[192,384]{1,0:T(8,128)}, f32[96,192]{1,0:T(8,128)}...) custom-call(bf16[4,512,768]{2,1,0:T(8,128)(2,1)} %get-tuple-element., ...), custom_call_target="tpu_custom_call" | custom-call | tf_op jit(solution)/shard_map/finish/pallas_call | solution.py:1209
